TPU v7x, 256 devices: a whole 4x4x8 slice. The times are simulated.
256 devices in a mesh: user: 32 (over z, x), tp: 8 (over y, core).
Axes of the slice: x: 4, y: 4, z: 8, core: 2. Of those that a mesh axis runs over, the one named last changes fastest.
Arguments:
- cand_feats: bfloat16 [32768, 1024], P('user', 'tp'), may hold values from -6 to 6
- w_in: bfloat16 [1024, 2048], P(None, 'tp'), may hold values from -0.1875 to 0.1875
- w_out: bfloat16 [1024, 1024], P('tp'), may hold values from -0.1875 to 0.1875
- kv_cache: bfloat16 [2048, 128, 2048], P('user', None, 'tp'), may hold values from -6 to 6
- event_mask: int32 [2048, 128], P('user'), may hold values from 0 to 1, as said below
- block_counts: int32 [256], P('user'), may hold values from 1 to 8, as said below
- user_blocks: int32 [256, 8], P('user'), may hold values from 0 to 63, as said below
- send_slots: int32 [1024, 2], P('user'), may hold values from 0 to 63, as said below
- cand_user: int32 [32768], P('user'), may hold values from 0 to 7
Outputs:
- scored: bfloat16 [32768, 1024], P('user', 'tp')
Inputs may be any that keep to these rules, and one draw needn't show every extreme that they name: `block_counts`: on every index of the user axis some user has 8 blocks, and on one index every user has. For user u of the index r of the user axis and j < block_counts[r * 8 + u], user_blocks[r * 8 + u, j] = o * 2 + c says that block j of u's history is cached on index o, in its local row send_slots[o * 32 + r, c] of kv_cache and event_mask. These valid entries of one index's users are all different, and on one index they take all 64 values. Entries with j >= block_counts[u] are arbitrary. `send_slots`: the 32 rows of one holder o (rows o * 32 to o * 32 + 31) name each of its local rows 0 to 63 exactly once. `event_mask`: in every block of a user's history the first event is real.
All inputs are finite; a program needn't handle non-finite values.
Results may differ from a plain program's by a relative error of at most 0.013.
Values may be sent and summed in bfloat16 or wider, within the bound.
A program may use at most 128 MiB of HBM per device.

v0:
```python
import jax
import jax.numpy as jnp
from jax import lax
from jax.sharding import PartitionSpec as P

DH = 128
EVENTS = 128
norm_eps = 1e-06


def owner_users(block_count, block_table, slot_count):
    user_count, most_blocks = block_table.shape
    live_mask = jnp.arange(most_blocks, dtype=jnp.int32)[None, :] < block_count[:, None]
    slot_hit = (
        block_table[:, :, None] == jnp.arange(slot_count, dtype=jnp.int32)[None, None, :]
    ) & live_mask[:, :, None]
    user_label = jnp.arange(user_count, dtype=jnp.int32)[:, None, None] + 1
    return jnp.sum(jnp.where(slot_hit, user_label, 0), axis=(0, 1)) - 1


def attend(queries, users, key_pairs, marks, owners):
    row_count, heads_here = (queries.shape[0], queries.shape[1])
    block_rows = min(512, row_count)
    pair_rows = key_pairs.reshape(-1, heads_here, 2, DH)
    key_rows = pair_rows[:, :, 0, :]
    value_rows = pair_rows[:, :, 1, :]
    live_mask = marks.reshape(-1, EVENTS).astype(jnp.float32)
    owner_label = owners.astype(jnp.float32)

    def one_block(packed):
        query_block, user_block = packed
        same_user = (user_block.astype(jnp.float32)[:, None] == owner_label[None, :]).astype(
            jnp.float32
        )
        weights = (same_user[:, :, None] * live_mask[None]).reshape(query_block.shape[0], -1)
        scores = jnp.einsum(
            "rhd,ehd->hre", query_block, key_rows, preferred_element_type=jnp.float32
        ) * DH ** (-0.5)
        attn_weights = (jax.nn.silu(scores) * weights[None]).astype(jnp.bfloat16)
        return jnp.einsum(
            "hre,ehd->rhd", attn_weights, value_rows, preferred_element_type=jnp.float32
        )

    result = lax.map(
        one_block, (queries.reshape(-1, block_rows, heads_here, DH), users.reshape(-1, block_rows))
    )
    return result.reshape(row_count, heads_here, DH)


def per_device(
    cand_feats, w_in, w_out, kv_cache, event_mask, block_counts, user_blocks, send_slots, cand_user
):
    row_count = cand_feats.shape[0]
    heads_here = w_out.shape[0] // DH
    projected = jnp.dot(
        lax.all_gather(cand_feats, "tp", axis=1, tiled=True),
        w_in,
        preferred_element_type=jnp.float32,
    )
    activated = jax.nn.silu(projected).reshape(row_count, heads_here, 2, DH)
    queries = activated[:, :, 0, :].astype(jnp.bfloat16)
    gates = activated[:, :, 1, :].astype(jnp.bfloat16)
    peer_count = lax.axis_size("user")
    capacity = send_slots.shape[1]
    slot_users = owner_users(block_counts, user_blocks, peer_count * capacity)
    picked = send_slots.reshape(-1)
    outgoing = kv_cache[picked].reshape(peer_count, capacity, EVENTS, kv_cache.shape[2])
    out_marks = event_mask[picked].reshape(peer_count, capacity, EVENTS).astype(jnp.bfloat16)
    arrived, arrived_marks = (
        lax.all_to_all(outgoing, "user", split_axis=0, concat_axis=0, tiled=True),
        lax.all_to_all(out_marks, "user", split_axis=0, concat_axis=0, tiled=True),
    )
    attended = attend(queries, cand_user, arrived, arrived_marks, slot_users)
    normed = (
        attended
        * lax.rsqrt(jnp.mean(attended * attended, axis=-1, keepdims=True) + norm_eps)
        * gates.astype(jnp.float32)
    )
    hidden = normed.astype(jnp.bfloat16).reshape(row_count, heads_here * DH)
    head_terms = jnp.dot(hidden, w_out, preferred_element_type=jnp.float32)
    summed = lax.psum_scatter(
        head_terms.astype(jnp.bfloat16), "tp", scatter_dimension=1, tiled=True
    ).astype(jnp.float32)
    return (cand_feats.astype(jnp.float32) + summed).astype(jnp.bfloat16)


def solution(mesh):
    in_specs = (
        P("user", "tp"),
        P(None, "tp"),
        P("tp", None),
        P("user", None, "tp"),
        P("user", None),
        P("user"),
        P("user", None),
        P("user", None),
        P("user"),
    )
    out_specs = P("user", "tp")
    return jax.shard_map(
        per_device, mesh=mesh, in_specs=in_specs, out_specs=out_specs, check_vma=False
    )
```

profile of v0, /device:TPU:2, one launch (start us, length us, event | category | flops | bytes accessed | tf_op | source)
XLA Modules:
  0.0 248.5 jit_solution(2677720347667687180)
XLA Ops:
  6.5 0.8 copy.22
  7.4 0.1 reshape.201
  7.5 1.4 gather_fusion.1
  8.8 0.6 convert_element_type.84
  9.5 11.6 %all-to-all-start.1 = ((bf16[32,2,128]{2,1,0:T(2,128)(2,1)}), bf16[32,2,128]{2,1,0:T(2,128)(2,1)S(1)}, u32[]{:S(2)}, u32[]{:S(2)}) async-start(bf16[32,2,128]{2,1,0:T(2,128)(2,1)} %bitcast.14), calls=%async_computation.1 | async-start | bytes 32768 | tf_op jit(solution)/shard_map/all_to_all | solution.py:71
  21.1 5.0 %gather_fusion = bf16[64,128,256]{2,1,0:T(8,128)(2,1)} fusion(bf16[64,128,256]{2,1,0:T(8,128)(2,1)} %param.14, s32[1024]{0:T(1024)S(1)} %pad_clamp_fusion), kind=kCustom, calls=%fused_computation | custom fusion | bytes 8388864 | tf_op jit(solution)/shard_map/gather | solution.py:67
  26.0 3.5 %all-to-all-done.1 = bf16[32,2,128]{2,1,0:T(2,128)(2,1)S(1)} async-done(((bf16[32,2,128]{2,1,0:T(2,128)(2,1)}), bf16[32,2,128]{2,1,0:T(2,128)(2,1)S(1)}, u32[]{:S(2)}, u32[]{:S(2)}) %all-to-all-start.1) | async-done | bytes 16416 | tf_op jit(solution)/shard_map/all_to_all | solution.py:71
  29.5 6.5 %all-to-all-start = ((bf16[32,2,128,256]{3,2,1,0:T(8,128)(2,1)}), bf16[32,2,128,256]{3,2,1,0:T(8,128)(2,1)}, u32[]{:S(2)}, u32[]{:S(2)}) async-start(bf16[32,2,128,256]{3,2,1,0:T(8,128)(2,1)} %bitcast.92), calls=%async_computation | async-start | bytes 8388608 | tf_op jit(solution)/shard_map/all_to_all | solution.py:70
  36.1 0.7 all-gather.2.cloned.1.call-update
  37.0 0.1 select_reduce_fusion
  37.1 32.6 %all-gather.2.cloned.1.call-done = bf16[1024,1024]{1,0:T(8,128)(2,1)} async-done(((bf16[1024,128]{1,0:T(8,128)(2,1)}), bf16[1024,1024]{1,0:T(8,128)(2,1)}) %all-gather.2.cloned.1.call-update) | async-done | bytes 2097168 | tf_op jit(solution)/shard_map/all_gather | solution.py:56
  69.7 2.5 %multiply_convert_fusion = bf16[1024,256]{0,1:T(8,128)(2,1)S(1)} fusion(bf16[1024,1024]{1,0:T(8,128)(2,1)} %all-gather.2.cloned.1.call-done, bf16[1024,256]{1,0:T(8,128)(2,1)S(1)} %copy-done), kind=kOutput, calls=%fused_computation.20 | convolution fusion | flops 538181632 | bytes 3145728 | tf_op jit(solution)/shard_map/dot_general | solution.py:55
  72.2 0.8 copy-done.2
  73.0 0.8 copy.29
  73.8 55.0 %all-to-all-done = bf16[32,2,128,256]{3,2,1,0:T(8,128)(2,1)} async-done(((bf16[32,2,128,256]{3,2,1,0:T(8,128)(2,1)}), bf16[32,2,128,256]{3,2,1,0:T(8,128)(2,1)}, u32[]{:S(2)}, u32[]{:S(2)}) %all-to-all-start) | async-done | bytes 4194336 | tf_op jit(solution)/shard_map/all_to_all | solution.py:70
  128.9 7.0 %reshape.203 = bf16[8192,1,2,128]{3,2,0,1:T(2,128)(2,1)} reshape(bf16[32,2,128,256]{3,2,1,0:T(8,128)(2,1)} %all-to-all-done) | data formatting | bytes 8388608 | tf_op jit(solution)/shard_map/reshape | solution.py:24
  135.8 8.9 %fusion.29 = (bf16[8192,1,1,128]{3,2,0,1:T(2,128)(2,1)S(1)}, bf16[8192,1,1,128]{3,2,0,1:T(2,128)(2,1)S(1)}) fusion(bf16[8192,1,2,128]{3,2,0,1:T(2,128)(2,1)} %reshape.203), kind=kLoop, calls=%fused_computation.37 | loop fusion | bytes 8388608 | tf_op jit(solution)/shard_map/slice | solution.py:26
  144.7 1.9 copy_bitcast_fusion
  146.6 53.2 %while.10 = (s32[]{:T(128)}, f32[2,512,1,128]{3,1,2,0:T(8,128)S(1)}, bf16[2,512,1,128]{3,1,2,0:T(8,128)(2,1)}, bf16[8192,1,128]{2,0,1:T(8,128)(2,1)}, s32[2,512]...) while((s32[]{:T(128)}, ...), condition=%wide.region_2.3_spmd, body=%wide.region_1.2_spmd.sunk | while | flops 2181104128 | bytes 38444384 | solution.py:44
  146.6 0.1 compare_convert_fusion.2
  146.8 7.0 %mul.127 = f32[512,64,128]{2,1,0:T(8,128)} broadcast(f32[512,64]{1,0:T(8,128)S(1)} %compare_convert_fusion.2), dimensions={0,1} | broadcast | bytes 16908288 | tf_op jit(solution)/shard_map/while/body/eval_jaxpr/mul | solution.py:35
  153.8 19.4 %fusion.40 = f32[2,512,1,128]{3,1,2,0:T(8,128)S(1)} fusion(f32[2,512,1,128]{3,1,2,0:T(8,128)S(1)} %get-tuple-element.151, s32[]{:T(128)} %get-tuple-element.150, bf16[8192,1,128]{2,0,1:T(8,128)(2,1)S(1)} %get-tuple-element.166, f32[64,8,64,128]{3,2,1,0:T(8,128)} %bitcast.91, f32[8192]{0:T(1024)S(1)} %bitcast.101, ...), kind=kOutput, calls=%fused_computation.9.clone.1 | convolution fusion | flops 2181038080 | bytes 21398528 | tf_op jit(solution)/shard_map/while/body/eval_jaxpr/hre,ehd->rhd/dot_general | solution.py:40
  173.2 0.1 compare_convert_fusion.2
  173.4 7.0 %mul.127 = f32[512,64,128]{2,1,0:T(8,128)} broadcast(f32[512,64]{1,0:T(8,128)S(1)} %compare_convert_fusion.2), dimensions={0,1} | broadcast | bytes 16908288 | tf_op jit(solution)/shard_map/while/body/eval_jaxpr/mul | solution.py:35
  180.4 19.4 %fusion.40 = f32[2,512,1,128]{3,1,2,0:T(8,128)S(1)} fusion(f32[2,512,1,128]{3,1,2,0:T(8,128)S(1)} %get-tuple-element.151, s32[]{:T(128)} %get-tuple-element.150, bf16[8192,1,128]{2,0,1:T(8,128)(2,1)S(1)} %get-tuple-element.166, f32[64,8,64,128]{3,2,1,0:T(8,128)} %bitcast.91, f32[8192]{0:T(1024)S(1)} %bitcast.101, ...), kind=kOutput, calls=%fused_computation.9.clone.1 | convolution fusion | flops 2181038080 | bytes 21398528 | tf_op jit(solution)/shard_map/while/body/eval_jaxpr/hre,ehd->rhd/dot_general | solution.py:40
  199.8 0.2 multiply_reduce_fusion
  200.1 0.2 copy.24
  200.3 1.7 convolution_convert_fusion
  202.0 2.6 %copy.25 = bf16[1024,1024]{0,1:T(8,128)(2,1)} copy(bf16[1024,1024]{1,0:T(8,128)(2,1)S(1)} %convolution_convert_fusion) | data formatting | bytes 4194304
  204.6 35.1 %reduce-scatter.4.cloned.1.call-done = bf16[128,1024]{1,0:T(8,128)(2,1)} async-done(((bf16[1024,1024]{1,0:T(8,128)(2,1)}), bf16[128,1024]{1,0:T(8,128)(2,1)}) %reduce-scatter.4.cloned.1.call-update) | async-done | bytes 262160
  239.8 1.1 copy.26
  240.9 0.8 add_convert_fusion
  (29 shorter events, 0.3 us)
Async XLA Ops:
  6.5 63.1 %copy-start = (bf16[1024,256]{1,0:T(8,128)(2,1)S(1)}, bf16[1024,256]{1,0:T(8,128)(2,1)}, u32[]{:S(2)}) copy-start(bf16[1024,256]{1,0:T(8,128)(2,1)} %param.12) | copy-start | bytes 1572868
  9.5 20.1 %all-to-all-start.1 = ((bf16[32,2,128]{2,1,0:T(2,128)(2,1)}), bf16[32,2,128]{2,1,0:T(2,128)(2,1)S(1)}, u32[]{:S(2)}, u32[]{:S(2)}) async-start(bf16[32,2,128]{2,1,0:T(2,128)(2,1)} %bitcast.14), calls=%async_computation.1 | async-start | bytes 32768 | tf_op jit(solution)/shard_map/all_to_all | solution.py:71
  29.5 7.3 %copy-start.5 = (s32[1024]{0:T(1024)S(1)}, s32[1024]{0:T(1024)}, u32[]{:S(2)}) copy-start(s32[1024]{0:T(1024)} %param.19) | copy-start | bytes 12292
  29.5 7.3 %copy-start.6 = (s32[8]{0:T(128)S(1)}, s32[8]{0:T(128)}, u32[]{:S(2)}) copy-start(s32[8]{0:T(128)} %param.16) | copy-start | bytes 100
  29.5 7.4 %copy-start.4 = (s32[8,8]{1,0:T(8,128)S(1)}, s32[8,8]{1,0:T(8,128)}, u32[]{:S(2)}) copy-start(s32[8,8]{1,0:T(8,128)} %param.17) | copy-start | bytes 772
  29.5 99.3 %all-to-all-start = ((bf16[32,2,128,256]{3,2,1,0:T(8,128)(2,1)}), bf16[32,2,128,256]{3,2,1,0:T(8,128)(2,1)}, u32[]{:S(2)}, u32[]{:S(2)}) async-start(bf16[32,2,128,256]{3,2,1,0:T(8,128)(2,1)} %bitcast.92), calls=%async_computation | async-start | bytes 8388608 | tf_op jit(solution)/shard_map/all_to_all | solution.py:70
  36.0 33.6 %all-gather.2.cloned.1.call-start = ((), (), s32[]{:S(2)}) async-start(), calls=%async_computation.3 | async-start | bytes 2359296 | tf_op jit(solution)/shard_map/all_gather | solution.py:56
  36.8 203.0 %reduce-scatter.4.cloned.1.call-start = ((), (), s32[]{:S(2)}) async-start(), calls=%async_computation.4 | async-start | bytes 2359296
  72.2 0.8 copy-start.2
  146.6 53.7 %copy-start.3 = (bf16[128,1024]{1,0:T(8,128)(2,1)S(1)}, bf16[128,1024]{1,0:T(8,128)(2,1)}, u32[]{:S(2)}) copy-start(bf16[128,1024]{1,0:T(8,128)(2,1)} %param.13) | copy-start | bytes 786436
  202.0 38.9 %copy-start.1 = (bf16[1024,128]{1,0:T(8,128)(2,1)S(1)}, bf16[1024,128]{1,0:T(8,128)(2,1)}, u32[]{:S(2)}) copy-start(bf16[1024,128]{1,0:T(8,128)(2,1)} %param.11) | copy-start | bytes 786436
Sparse Core Ops, SparseCore 0:
  38.7 30.9 all-gather.1
  204.7 34.9 reduce-scatter.3
where the time goes:
time: 249 us
  waiting for transfers between devices  127 us (51%)
  local copies, waits for them, and re-layouts  44.6 us (18%)
  matrix products  43 us (17%)
  starting transfers between devices  18.2 us (7%)
  between operations  13.6 us (5%)
    all_to_all x1, waiting for transfers between devices, per_device(): lax.all_to_all(outgoing, 'user', split_axis=0, concat_axis=0, tiled=True)  55 us
    dot_general x2, matrix products, one_block(): jnp.einsum('hre,ehd->rhd', attn_weights, value_rows, preferred_element_ty...  38.9 us
    unnamed x3, waiting for transfers between devices  35.8 us
    all_gather x1, waiting for transfers between devices, per_device(): lax.all_gather(cand_feats, 'tp', axis=1, tiled=True)  32.6 us
    mul x2, local copies, waits for them, and re-layouts, one_block(): same_user[:, :, None] * live_mask[None]  14 us
    all_to_all x1, starting transfers between devices, per_device(): lax.all_to_all(out_marks, 'user', split_axis=0, concat_axis=0, tiled=True)  11.6 us
    slice x1, local copies, waits for them, and re-layouts, attend(): value_rows = pair_rows[:, :, 1, :]  8.89 us
    unnamed x20, local copies, waits for them, and re-layouts  8.03 us
  transfers between devices with their start and end apart: 4, of which 4 were waited for; matrix products, arithmetic and copies ran while one was open for 3% of the time, Pallas kernels for 0%

commit v1 on v0

--- a/solution.py
+++ b/solution.py
@@ -53,7 +53,15 @@
     row_count = cand_feats.shape[0]
     heads_here = w_out.shape[0] // DH
     projected = jnp.dot(
-        lax.all_gather(cand_feats, "tp", axis=1, tiled=True),
+        jnp.concatenate(
+            jax.lax.all_to_all(
+                jnp.stack([cand_feats] * jax.lax.axis_size("tp")),
+                split_axis=0,
+                axis_name="tp",
+                concat_axis=0,
+            ),
+            1,
+        ),
         w_in,
         preferred_element_type=jnp.float32,
     )

time: 249 us -> 282 us (1.13)
  waiting for transfers between devices: 127 us -> 154 us
  starting transfers between devices: 18.2 us -> 22.1 us
  local copies, waits for them, and re-layouts: 44.6 us -> 48 us
    all_to_all x1, waiting for transfers between devices: 55 us -> 93.9 us  [per_device(): lax.all_to_all(outgoing, 'user', split_axis=0, concat_axis=0, tiled=True)]
    all_gather x1 -> x0, waiting for transfers between devices: 32.6 us -> none  [per_device(): lax.all_gather(cand_feats, 'tp', axis=1, tiled=True)]
    all_to_all x0 -> x1, waiting for transfers between devices: none -> 22.2 us  [per_device(): jax.lax.all_to_all(jnp.stack([cand_feats] * jax.lax.axis_size('tp')), spl...]
    unnamed x3 -> x2, waiting for transfers between devices: 35.8 us -> 30.2 us
    all_to_all x0 -> x1, starting transfers between devices: none -> 4.47 us  [per_device(): jax.lax.all_to_all(jnp.stack([cand_feats] * jax.lax.axis_size('tp')), spl...]
    all_to_all x1, waiting for transfers between devices: 3.48 us -> 7.35 us  [per_device(): lax.all_to_all(out_marks, 'user', split_axis=0, concat_axis=0, tiled=True)]
    unnamed x20 -> x21, local copies, waits for them, and re-layouts: 8.03 us -> 9.12 us
where the time goes in v1:
time: 282 us; the launch traced here: 281 us
  waiting for transfers between devices  154 us (55%)
  local copies, waits for them, and re-layouts  48 us (17%)
  matrix products  41.6 us (15%)
  starting transfers between devices  22.1 us (8%)
  between operations  13.6 us (5%)
    all_to_all x1, waiting for transfers between devices, per_device(): lax.all_to_all(outgoing, 'user', split_axis=0, concat_axis=0, tiled=True)  93.9 us
    dot_general x2, matrix products, one_block(): jnp.einsum('hre,ehd->rhd', attn_weights, value_rows, preferred_element_ty...  38.9 us
    unnamed x2, waiting for transfers between devices  30.2 us
    all_to_all x1, waiting for transfers between devices, per_device(): jax.lax.all_to_all(jnp.stack([cand_feats] * jax.lax.axis_size('tp')), spl...  22.2 us
    mul x2, local copies, waits for them, and re-layouts, one_block(): same_user[:, :, None] * live_mask[None]  14.1 us
    all_to_all x1, starting transfers between devices, per_device(): lax.all_to_all(out_marks, 'user', split_axis=0, concat_axis=0, tiled=True)  11.6 us
    unnamed x21, local copies, waits for them, and re-layouts  9.12 us
    slice x1, local copies, waits for them, and re-layouts, attend(): value_rows = pair_rows[:, :, 1, :]  8.82 us
  transfers between devices with their start and end apart: 4, of which 4 were waited for; matrix products, arithmetic and copies ran while one was open for 3% of the time, Pallas kernels for 0%

profile of v1, /device:TPU:2, one launch (start us, length us, event | category | flops | bytes accessed | tf_op | source)
XLA Modules:
  0.0 281.2 jit_solution(5782591521710516762)
XLA Ops:
  6.5 0.8 copy.25
  7.5 1.4 gather_fusion.1
  8.8 0.6 convert_element_type.84
  9.5 11.6 %all-to-all-start.2 = ((bf16[32,2,128]{2,1,0:T(2,128)(2,1)}), bf16[32,2,128]{2,1,0:T(2,128)(2,1)S(1)}, u32[]{:S(2)}, u32[]{:S(2)}) async-start(bf16[32,2,128]{2,1,0:T(2,128)(2,1)} %bitcast.16), calls=%async_computation.2 | async-start | bytes 32768 | tf_op jit(solution)/shard_map/all_to_all | solution.py:79
  21.1 1.1 copy.23
  22.2 7.4 %all-to-all-done.2 = bf16[32,2,128]{2,1,0:T(2,128)(2,1)S(1)} async-done(((bf16[32,2,128]{2,1,0:T(2,128)(2,1)}), bf16[32,2,128]{2,1,0:T(2,128)(2,1)S(1)}, u32[]{:S(2)}, u32[]{:S(2)}) %all-to-all-start.2) | async-done | bytes 16416 | tf_op jit(solution)/shard_map/all_to_all | solution.py:79
  29.5 1.6 stack.2
  31.1 4.5 %all-to-all-start = ((bf16[8,1024,128]{1,2,0:T(8,128)(2,1)}), bf16[8,1024,128]{1,2,0:T(8,128)(2,1)S(1)}, u32[]{:S(2)}, u32[]{:S(2)}) async-start(bf16[8,1024,128]{1,2,0:T(8,128)(2,1)} %stack.2), calls=%async_computation | async-start | bytes 4194304 | tf_op jit(solution)/shard_map/all_to_all | solution.py:57
  35.6 5.0 %gather_fusion = bf16[64,128,256]{2,1,0:T(8,128)(2,1)} fusion(bf16[64,128,256]{2,1,0:T(8,128)(2,1)} %param.14, s32[1024]{0:T(1024)S(1)} %pad_clamp_fusion), kind=kCustom, calls=%fused_computation | custom fusion | bytes 8388864 | tf_op jit(solution)/shard_map/gather | solution.py:75
  40.6 22.2 %all-to-all-done = bf16[8,1024,128]{1,2,0:T(8,128)(2,1)S(1)} async-done(((bf16[8,1024,128]{1,2,0:T(8,128)(2,1)}), bf16[8,1024,128]{1,2,0:T(8,128)(2,1)S(1)}, u32[]{:S(2)}, u32[]{:S(2)}) %all-to-all-start) | async-done | bytes 2097184 | tf_op jit(solution)/shard_map/all_to_all | solution.py:57
  62.8 6.0 %all-to-all-start.1 = ((bf16[32,2,128,256]{3,2,1,0:T(8,128)(2,1)}), bf16[32,2,128,256]{3,2,1,0:T(8,128)(2,1)}, u32[]{:S(2)}, u32[]{:S(2)}) async-start(bf16[32,2,128,256]{3,2,1,0:T(8,128)(2,1)} %bitcast.95), calls=%async_computation.1 | async-start | bytes 8388608 | tf_op jit(solution)/shard_map/all_to_all | solution.py:78
  69.1 0.9 multiply_convert_fusion
  70.1 0.8 copy-done.2
  70.9 0.8 copy.32
  71.7 93.9 %all-to-all-done.1 = bf16[32,2,128,256]{3,2,1,0:T(8,128)(2,1)} async-done(((bf16[32,2,128,256]{3,2,1,0:T(8,128)(2,1)}), bf16[32,2,128,256]{3,2,1,0:T(8,128)(2,1)}, u32[]{:S(2)}, u32[]{:S(2)}) %all-to-all-start.1) | async-done | bytes 4194336 | tf_op jit(solution)/shard_map/all_to_all | solution.py:78
  165.6 7.0 %reshape.213 = bf16[8192,1,2,128]{3,2,0,1:T(2,128)(2,1)} reshape(bf16[32,2,128,256]{3,2,1,0:T(8,128)(2,1)} %all-to-all-done.1) | data formatting | bytes 8388608 | tf_op jit(solution)/shard_map/reshape | solution.py:24
  172.6 8.8 %fusion.29 = (bf16[8192,1,1,128]{3,2,0,1:T(2,128)(2,1)S(1)}, bf16[8192,1,1,128]{3,2,0,1:T(2,128)(2,1)S(1)}) fusion(bf16[8192,1,2,128]{3,2,0,1:T(2,128)(2,1)} %reshape.213), kind=kLoop, calls=%fused_computation.37 | loop fusion | bytes 8388608 | tf_op jit(solution)/shard_map/slice | solution.py:26
  181.4 1.9 copy_bitcast_fusion
  183.3 53.2 %while.10 = (s32[]{:T(128)}, f32[2,512,1,128]{3,1,2,0:T(8,128)S(1)}, bf16[2,512,1,128]{3,1,2,0:T(8,128)(2,1)}, bf16[8192,1,128]{2,0,1:T(8,128)(2,1)}, s32[2,512]...) while((s32[]{:T(128)}, ...), condition=%wide.region_2.3_spmd, body=%wide.region_1.2_spmd.sunk | while | flops 2181104128 | bytes 38444384 | solution.py:44
  183.3 0.1 compare_convert_fusion.2
  183.4 7.0 %mul.127 = f32[512,64,128]{2,1,0:T(8,128)} broadcast(f32[512,64]{1,0:T(8,128)S(1)} %compare_convert_fusion.2), dimensions={0,1} | broadcast | bytes 16908288 | tf_op jit(solution)/shard_map/while/body/eval_jaxpr/mul | solution.py:35
  190.5 19.4 %fusion.40 = f32[2,512,1,128]{3,1,2,0:T(8,128)S(1)} fusion(f32[2,512,1,128]{3,1,2,0:T(8,128)S(1)} %get-tuple-element.151, s32[]{:T(128)} %get-tuple-element.150, bf16[8192,1,128]{2,0,1:T(8,128)(2,1)S(1)} %get-tuple-element.166, f32[64,8,64,128]{3,2,1,0:T(8,128)} %bitcast.94, f32[8192]{0:T(1024)S(1)} %bitcast.105, ...), kind=kOutput, calls=%fused_computation.9.clone.1 | convolution fusion | flops 2181038080 | bytes 21398528 | tf_op jit(solution)/shard_map/while/body/eval_jaxpr/hre,ehd->rhd/dot_general | solution.py:40
  209.9 0.1 compare_convert_fusion.2
  210.1 7.0 %mul.127 = f32[512,64,128]{2,1,0:T(8,128)} broadcast(f32[512,64]{1,0:T(8,128)S(1)} %compare_convert_fusion.2), dimensions={0,1} | broadcast | bytes 16908288 | tf_op jit(solution)/shard_map/while/body/eval_jaxpr/mul | solution.py:35
  217.1 19.4 %fusion.40 = f32[2,512,1,128]{3,1,2,0:T(8,128)S(1)} fusion(f32[2,512,1,128]{3,1,2,0:T(8,128)S(1)} %get-tuple-element.151, s32[]{:T(128)} %get-tuple-element.150, bf16[8192,1,128]{2,0,1:T(8,128)(2,1)S(1)} %get-tuple-element.166, f32[64,8,64,128]{3,2,1,0:T(8,128)} %bitcast.94, f32[8192]{0:T(1024)S(1)} %bitcast.105, ...), kind=kOutput, calls=%fused_computation.9.clone.1 | convolution fusion | flops 2181038080 | bytes 21398528 | tf_op jit(solution)/shard_map/while/body/eval_jaxpr/hre,ehd->rhd/dot_general | solution.py:40
  236.5 0.2 multiply_reduce_fusion
  236.8 1.0 copy.27
  237.8 1.8 convolution_convert_fusion
  239.7 2.6 copy.28
  242.3 30.2 %reduce-scatter.4.cloned.1.call-done = bf16[128,1024]{1,0:T(8,128)(2,1)} async-done(((bf16[1024,1024]{1,0:T(8,128)(2,1)}), bf16[128,1024]{1,0:T(8,128)(2,1)}) %reduce-scatter.4.cloned.1.call-update) | async-done | bytes 262160
  272.4 1.1 copy.29
  273.6 0.8 add_convert_fusion
  (30 shorter events, 0.4 us)
Async XLA Ops:
  6.5 62.6 %copy-start = (bf16[1024,256]{1,0:T(8,128)(2,1)S(1)}, bf16[1024,256]{1,0:T(8,128)(2,1)}, u32[]{:S(2)}) copy-start(bf16[1024,256]{1,0:T(8,128)(2,1)} %param.12) | copy-start | bytes 1572868
  9.5 20.1 %all-to-all-start.2 = ((bf16[32,2,128]{2,1,0:T(2,128)(2,1)}), bf16[32,2,128]{2,1,0:T(2,128)(2,1)S(1)}, u32[]{:S(2)}, u32[]{:S(2)}) async-start(bf16[32,2,128]{2,1,0:T(2,128)(2,1)} %bitcast.16), calls=%async_computation.2 | async-start | bytes 32768 | tf_op jit(solution)/shard_map/all_to_all | solution.py:79
  31.1 31.7 %all-to-all-start = ((bf16[8,1024,128]{1,2,0:T(8,128)(2,1)}), bf16[8,1024,128]{1,2,0:T(8,128)(2,1)S(1)}, u32[]{:S(2)}, u32[]{:S(2)}) async-start(bf16[8,1024,128]{1,2,0:T(8,128)(2,1)} %stack.2), calls=%async_computation | async-start | bytes 4194304 | tf_op jit(solution)/shard_map/all_to_all | solution.py:57
  62.8 6.1 %copy-start.5 = (s32[1024]{0:T(1024)S(1)}, s32[1024]{0:T(1024)}, u32[]{:S(2)}) copy-start(s32[1024]{0:T(1024)} %param.19) | copy-start | bytes 12292
  62.8 6.1 %copy-start.6 = (s32[8]{0:T(128)S(1)}, s32[8]{0:T(128)}, u32[]{:S(2)}) copy-start(s32[8]{0:T(128)} %param.16) | copy-start | bytes 100
  62.8 6.2 %copy-start.4 = (s32[8,8]{1,0:T(8,128)S(1)}, s32[8,8]{1,0:T(8,128)}, u32[]{:S(2)}) copy-start(s32[8,8]{1,0:T(8,128)} %param.17) | copy-start | bytes 772
  62.8 102.8 %all-to-all-start.1 = ((bf16[32,2,128,256]{3,2,1,0:T(8,128)(2,1)}), bf16[32,2,128,256]{3,2,1,0:T(8,128)(2,1)}, u32[]{:S(2)}, u32[]{:S(2)}) async-start(bf16[32,2,128,256]{3,2,1,0:T(8,128)(2,1)} %bitcast.95), calls=%async_computation.1 | async-start | bytes 8388608 | tf_op jit(solution)/shard_map/all_to_all | solution.py:78
  68.8 203.6 %reduce-scatter.4.cloned.1.call-start = ((), (), s32[]{:S(2)}) async-start(), calls=%async_computation.4 | async-start | bytes 2359296
  70.1 0.8 copy-start.2
  183.3 54.5 %copy-start.3 = (bf16[128,1024]{1,0:T(8,128)(2,1)S(1)}, bf16[128,1024]{1,0:T(8,128)(2,1)}, u32[]{:S(2)}) copy-start(bf16[128,1024]{1,0:T(8,128)(2,1)} %param.13) | copy-start | bytes 786436
  239.7 33.9 %copy-start.1 = (bf16[1024,128]{1,0:T(8,128)(2,1)S(1)}, bf16[1024,128]{1,0:T(8,128)(2,1)}, u32[]{:S(2)}) copy-start(bf16[1024,128]{1,0:T(8,128)(2,1)} %param.11) | copy-start | bytes 786436
Sparse Core Ops, SparseCore 0:
  242.4 29.9 reduce-scatter.3
